TPU v7x, 512 devices: a whole 4x4x16 slice. The times are simulated.
512 devices in a mesh: place: 16 (over y, x_hi, core), tok: 32 (over z, x_lo).
Axes of the slice: x: 4 (x_hi: 2, x_lo: 2; x = x_hi * 2 + x_lo), y: 4, z: 16, core: 2. Of those that a mesh axis runs over, the one named last changes fastest.
Arguments:
- tokens: bfloat16 [8192, 2048], P('tok', 'place'), may hold values from -6 to 6
- mod_shift: float32 [2048], replicated, may hold values from -3 to 3
- mod_scale: float32 [2048], replicated, may hold values from -2.5 to 2.5
- res_gate: float32 [2048], replicated, may hold values from 0.5 to 1.5
- weight_in: bfloat16 [32, 2048, 8192], P('tok', None, 'place'), may hold values from -0.125 to 0.125
- weight_out: bfloat16 [32, 8192, 2048], P('tok', 'place'), may hold values from -0.09375 to 0.09375
- expert_slot: int32 [32], replicated, may hold values from 0 to 31, each once
- routes: int32 [8192, 2], P('tok'), may hold values from 0 to 31, all different within a row; in each aligned block of 256 rows (0 to 255, 256 to 511, ...) at most 24 rows name the same one
- gate_fixed: int32 [8192, 2], P('tok'), may hold values from 1 to 65535
Outputs:
- mixed: bfloat16 [8192, 2048], P('tok', 'place')
Inputs may be any that keep to these rules, and one draw needn't show every extreme that they name: `routes`: among the 256 tokens of one index of tok (aligned blocks of rows), no expert is named by more than 24 rows, a bound that some block reaches; each row names two different experts. A permutation: expert e's weights are slot expert_slot[e] of weight_in and weight_out.
All inputs are finite; a program needn't handle non-finite values.
Results may differ from a plain program's by a relative error of at most 0.013.
Values may be sent and summed in bfloat16 or wider, within the bound.
A program may use at most 64 MiB of HBM per device.

v0:
```python
import jax
import jax.numpy as jnp
from jax import lax
from jax.sharding import PartitionSpec as P

D = 2048
CAP = 24


def normalize(as_float, row_total, row_squares, mod_shift, mod_scale):
    row_mean = row_total / D
    inverse = lax.rsqrt(row_squares / D - row_mean * row_mean + 1e-06)
    return (
        (as_float - row_mean) * inverse * (1.0 + mod_scale[None, :]) + mod_shift[None, :]
    ).astype(jnp.bfloat16)


def shards(
    tokens, mod_shift, mod_scale, res_gate, weight_in, weight_out, expert_slot, routes, gate_fixed
):
    tok_count = lax.axis_size("tok")
    tok_rows = tokens.shape[0]
    col_width = tokens.shape[1]
    column_start = lax.axis_index("place") * col_width
    gate_part = lax.dynamic_slice_in_dim(res_gate, column_start, col_width, 0)
    flat_routes = routes.reshape(-1)
    assigned = flat_routes.shape[0]
    experts = expert_slot.shape[0]
    slots_dev = weight_in.shape[0]
    catalog = jnp.arange(experts, dtype=jnp.int32)
    slot_of = jnp.sum(
        jnp.where(flat_routes[:, None] == catalog[None, :], expert_slot[None, :], 0), axis=1
    )
    slot_hot = (slot_of[:, None] == catalog[None, :]).astype(jnp.int32)
    earlier = jnp.cumsum(slot_hot, axis=0) - slot_hot
    bucket = slot_of * CAP + jnp.sum(earlier * slot_hot, axis=1)
    places = jnp.arange(experts * CAP, dtype=jnp.int32)
    numbered = jnp.arange(1, assigned + 1, dtype=jnp.int32)
    source = jnp.sum(jnp.where(places[:, None] == bucket[None, :], numbered[None, :], 0), axis=1)
    filled = source > 0
    token_index = jnp.maximum(source - 1, 0) // 2
    as_float = tokens.astype(jnp.float32)
    gathered = lax.all_gather(tokens, "place", axis=1, tiled=True).astype(jnp.float32)
    normed = normalize(
        gathered,
        jnp.sum(gathered, axis=1, keepdims=True),
        jnp.sum(gathered * gathered, axis=1, keepdims=True),
        mod_shift,
        mod_scale,
    )
    outgoing = jnp.where(filled[:, None], normed[token_index], jnp.zeros((), jnp.bfloat16))
    outgoing = outgoing.reshape(tok_count, slots_dev, CAP, D)
    arrived = lax.all_to_all(outgoing, "tok", split_axis=0, concat_axis=0, tiled=True)
    hidden = jnp.einsum("nscd,sdf->nscf", arrived, weight_in, preferred_element_type=jnp.float32)
    activated = jax.nn.gelu(hidden, approximate=True).astype(jnp.bfloat16)
    partial_value = jnp.einsum(
        "nscf,sfd->nscd", activated, weight_out, preferred_element_type=jnp.float32
    ).astype(jnp.bfloat16)
    returned = lax.all_to_all(partial_value, "tok", split_axis=0, concat_axis=0, tiled=True)
    expert_out = (
        lax.psum_scatter(returned, "place", scatter_dimension=3, tiled=True)
        .astype(jnp.float32)
        .astype(jnp.bfloat16)
    )
    per_assign = expert_out.reshape(experts * CAP, col_width)[bucket].astype(jnp.float32)
    gate_values = gate_fixed.astype(jnp.float32).reshape(-1) / 65536.0
    combined = jnp.sum((gate_values[:, None] * per_assign).reshape(tok_rows, 2, col_width), axis=1)
    return (as_float + gate_part[None, :] * combined).astype(jnp.bfloat16)


def solution(mesh):
    placed = (
        P("tok", "place"),
        P(),
        P(),
        P(),
        P("tok", None, "place"),
        P("tok", "place", None),
        P(),
        P("tok", None),
        P("tok", None),
    )
    return jax.shard_map(
        shards, mesh=mesh, in_specs=placed, out_specs=P("tok", "place"), check_vma=False
    )
```

profile of v0, /device:TPU:1, one launch (start us, length us, event | category | flops | bytes accessed | tf_op | source)
XLA Modules:
  0.0 547.7 jit_solution(12582313480044953009)
XLA Ops:
  6.5 0.0 copy-start
  6.5 0.7 all-gather.2.cloned.1.call-update
  7.3 0.0 reduce-scatter.4.cloned.1.call-start
  7.3 0.8 copy.21
  8.1 0.1 eq.52
  8.3 0.7 select_reduce_fusion.1
  9.0 1.2 reduce-window.6
  10.2 0.2 slice_reduce_fusion
  10.5 0.1 fusion.34
  10.6 0.2 select_reduce_fusion
  10.8 0.1 gt.11
  11.0 0.7 broadcast_add_fusion
  11.7 62.7 %all-gather.2.cloned.1.call-done = bf16[256,2048]{1,0:T(8,128)(2,1)} async-done(((bf16[256,128]{1,0:T(8,128)(2,1)}), bf16[256,2048]{1,0:T(8,128)(2,1)}) %all-gather.2.cloned.1.call-update) | async-done | bytes 1048592 | tf_op jit(solution)/shard_map/all_gather | solution.py:43
  74.4 1.7 convert_reduce_fusion
  76.1 1.7 fusion.6
  77.8 4.3 gather_fusion
  82.1 2.2 broadcast_select_fusion
  84.2 155.9 %all_to_all.10 = bf16[32,1,24,2048]{3,2,1,0:T(8,128)(2,1)} all-to-all(bf16[32,1,24,2048]{3,2,1,0:T(8,128)(2,1)S(1)} %broadcast_select_fusion), channel_id=1, replica_groups=mesh['place'=16,'tok'=32] {'tok'}, dimensions={0} | all-to-all | bytes 6291456 | tf_op jit(solution)/shard_map/all_to_all | solution.py:53
  240.1 8.0 %fusion.2 = bf16[32,1,24,2048]{3,2,1,0:T(8,128)(2,1)} fusion(bf16[1,512,2048]{2,1,0:T(8,128)(2,1)S(1)} %copy-done, bf16[1,2048,512]{2,1,0:T(8,128)(2,1)} %param.13, bf16[32,1,24,2048]{3,2,1,0:T(8,128)(2,1)} %all_to_all.10), kind=kOutput, calls=%fused_computation.9 | convolution fusion | flops 3226337280 | bytes 10485760 | tf_op jit(solution)/shard_map/nscf,sfd->nscd/dot_general | solution.py:56
  248.1 148.0 %all_to_all.11 = bf16[32,1,24,2048]{3,2,1,0:T(8,128)(2,1)} all-to-all(bf16[32,1,24,2048]{3,2,1,0:T(8,128)(2,1)} %fusion.2), channel_id=1, replica_groups=mesh['place'=16,'tok'=32] {'tok'}, dimensions={0} | all-to-all | bytes 6291456 | tf_op jit(solution)/shard_map/all_to_all | solution.py:59
  396.1 23.4 %copy.26 = bf16[32,1,24,2048]{2,0,1,3:T(8,128)(2,1)} copy(bf16[32,1,24,2048]{3,2,0,1:T(8,128)(2,1)} %bitcast.80) | data formatting | bytes 6291456
  419.5 24.1 %reshape.214 = bf16[2048,768]{1,0:T(8,128)(2,1)} reshape(bf16[2048,1,32,24]{3,2,1,0:T(8,128)(2,1)} %bitcast.79) | data formatting | bytes 6291456
  443.6 0.0 reduce-scatter.4.cloned.1.call-update
  443.6 0.7 copy-done.2
  444.3 0.1 copy.20
  444.4 0.8 dynamic_slice.3
  445.2 89.5 %reduce-scatter.4.cloned.1.call-done = bf16[128,768]{1,0:T(8,128)(2,1)} async-done(((bf16[2048,768]{1,0:T(8,128)(2,1)}), bf16[128,768]{1,0:T(8,128)(2,1)}) %reduce-scatter.4.cloned.1.call-update) | async-done | bytes 196624
  534.7 2.6 reshape.215
  537.3 1.1 copy.27
  538.4 1.3 gather_fusion.1
  539.7 0.4 fusion.31
  540.2 0.7 add_convert_fusion
  (17 shorter events, 0.1 us)
Async XLA Ops:
  6.5 233.6 %copy-start = (bf16[1,512,2048]{2,1,0:T(8,128)(2,1)S(1)}, bf16[1,512,2048]{2,1,0:T(8,128)(2,1)}, u32[]{:S(2)}) copy-start(bf16[1,512,2048]{2,1,0:T(8,128)(2,1)} %param.14) | copy-start | bytes 6291460
  6.5 67.8 %all-gather.2.cloned.1.call-start = ((), (), s32[]{:S(2)}) async-start(), calls=%async_computation.3 | async-start | bytes 1114112 | tf_op jit(solution)/shard_map/all_gather | solution.py:43
  7.3 527.4 %reduce-scatter.4.cloned.1.call-start = ((), (), s32[]{:S(2)}) async-start(), calls=%async_computation.4 | async-start | bytes 3342336
  443.6 0.7 copy-start.2
  444.3 95.9 %copy-start.1 = (bf16[256,128]{1,0:T(8,128)(2,1)S(1)}, bf16[256,128]{1,0:T(8,128)(2,1)}, u32[]{:S(2)}) copy-start(bf16[256,128]{1,0:T(8,128)(2,1)} %param.9) | copy-start | bytes 196612
Sparse Core Ops, SparseCore 0:
  10.6 63.7 all-gather.1
  443.7 90.8 reduce-scatter.3
where the time goes:
time: 549 us; the launch traced here: 548 us
  blocking collectives  304 us (55%)
  waiting for transfers between devices  153 us (28%)
  local copies, waits for them, and re-layouts  59.7 us (11%)
  between operations  13.5 us (2%)
  other arithmetic  9.68 us (2%)
  matrix products  7.99 us (1%)
    all_to_all x1, blocking collectives, shards(): lax.all_to_all(outgoing, 'tok', split_axis=0, concat_axis=0, tiled=True)  156 us
    all_to_all x1, blocking collectives, shards(): lax.all_to_all(partial_value, 'tok', split_axis=0, concat_axis=0, tiled=T...  148 us
    unnamed x3, waiting for transfers between devices  90.2 us
    all_gather x1, waiting for transfers between devices, shards(): lax.all_gather(tokens, 'place', axis=1, tiled=True).astype(jnp.float32)  62.7 us
    unnamed x11, local copies, waits for them, and re-layouts  52.7 us
  transfers between devices with their start and end apart: 2, of which 2 were waited for; matrix products, arithmetic and copies ran while one was open for 1% of the time, Pallas kernels for 0%

commit v1 on v0

v1 whole, which is shorter than its diff:
```python
import functools

import jax
import jax.numpy as jnp
from jax import lax
from jax.experimental import pallas as pl
from jax.experimental.pallas import tpu as pltpu
from jax.sharding import PartitionSpec as P

D = 2048
CAP = 24
CHUNKS = 1
CHIPS = 8
PLACES = 16
LANES = 128
WIDE = 256
MESH = pl.DeviceIdType.MESH
F32 = jnp.float32
BF16 = jnp.bfloat16


def remote(src, dst, send_sem, recv_sem, device):
    return pltpu.make_async_remote_copy(
        src_ref=src,
        dst_ref=dst,
        send_sem=send_sem,
        recv_sem=recv_sem,
        device_id=device,
        device_id_type=MESH,
    )


def to_rows(block):
    slots = block.shape[0]
    wide = block.astype(F32)
    halves = [wide[:, h * CAP : (h + 1) * CAP].reshape(slots * CAP, LANES) for h in range(2)]
    return jnp.concatenate(halves, axis=1).astype(BF16)


def to_messages(rows):
    slots = rows.shape[0] // CAP
    halves = [rows[:, h * LANES : (h + 1) * LANES].reshape(slots, CAP, LANES) for h in range(2)]
    return jnp.concatenate(halves, axis=1).astype(BF16)


def kernel(
    n_tok,
    tokens,
    shift,
    scale,
    gate,
    routes,
    fixed,
    catalog,
    w_in,
    w_out,
    out,
    tok2,
    stat_out,
    stat_in,
    sent_rows,
    got_rows,
    held,
    win,
    wout,
    hid,
    part_own,
    part_near,
    far_out,
    far_in,
    near_out,
    near_in,
    x_out,
    x_in,
    back_out,
    back_in,
    pick_hi,
    pick_lo,
    comb,
    comb_in,
    w_sem,
    one_send,
    one_recv,
    stat_send,
    stat_recv,
    disp_send,
    disp_recv,
    gat_send,
    gat_recv,
    red_send,
    red_recv,
    back_send,
    back_recv,
):
    place, tok = lax.axis_index("place"), lax.axis_index("tok")
    nz = n_tok // 2
    slots_chunk = nz // CHUNKS
    rows = slots_chunk * CAP
    half = rows // 2
    core, chip = lax.rem(place, 2), lax.div(place, 2)
    xh, y = lax.rem(chip, 2), lax.div(chip, 2)
    z, xl = lax.div(tok, 2), lax.rem(tok, 2)
    sibling = (place + 1 - 2 * core, tok)
    across = (place + 2 - 4 * xh, tok)
    y_right, y_left, y_far = lax.rem(y + 1, 4), lax.rem(y + 3, 4), lax.rem(y + 2, 4)
    right = (y_right * 4 + xh * 2 + core, tok)
    left = (y_left * 4 + xh * 2 + core, tok)

    def mate(offset):
        return (lax.rem(place + offset, PLACES), tok)

    def peer(dz):
        return (place, lax.rem(z + dz, nz) * 2 + lax.rem(xl + core, 2))

    def step_of(d):
        return jnp.where(lax.rem(d, 2) == 1, lax.div(d + 1, 2), lax.rem(nz - lax.div(d, 2), nz))

    def piece(y_of, a):
        return y_of * 2 + lax.rem(xh + 1 + a, 2)

    barrier = pltpu.get_barrier_semaphore()

    def greet_place(offset, carry):
        pl.semaphore_signal(barrier, inc=1, device_id=mate(offset), device_id_type=MESH)
        return carry

    def greet_tok(dz, carry):
        pl.semaphore_signal(barrier, inc=1, device_id=peer(dz), device_id_type=MESH)
        return carry

    lax.fori_loop(1, PLACES, greet_place, 0)
    lax.fori_loop(1, nz, greet_tok, 0)

    @pl.when(core == 1)
    def _():
        greet_tok(0, 0)

    load_in = pltpu.make_async_copy(w_in.at[0], win.at[core], w_sem.at[0])
    load_out = pltpu.make_async_copy(w_out.at[0], wout.at[core], w_sem.at[1])
    load_in.start()
    load_out.start()

    count = tokens.shape[0]
    eye = lax.broadcasted_iota(jnp.int32, (count, count), 0) == lax.broadcasted_iota(
        jnp.int32, (count, count), 1
    )

    def as_row(column):
        return jnp.sum(jnp.where(eye, column, 0.0), axis=0, keepdims=True)

    def as_column(row):
        return jnp.sum(jnp.where(eye, row, 0.0), axis=1, keepdims=True)

    own = tokens[...].astype(F32)
    total_row = as_row(jnp.sum(own, axis=1, keepdims=True))
    square_row = as_row(jnp.sum(own * own, axis=1, keepdims=True))
    lines = lax.broadcasted_iota(jnp.int32, (8, count), 0)
    stat_out[...] = jnp.where(lines == 0, total_row, jnp.where(lines == 1, square_row, 0.0))
    tok2[core] = tokens[...]

    pl.semaphore_wait(barrier, PLACES - 1 + nz - 1 + core)

    def stat_copy(offset):
        return remote(
            stat_out, stat_in.at[offset], stat_send.at[offset], stat_recv.at[offset], mate(offset)
        )

    def start_stat(offset, carry):
        stat_copy(offset).start()
        return carry

    lax.fori_loop(1, PLACES, start_stat, 0)
    tok_copy = remote(tokens, tok2.at[core], one_send.at[0], one_recv.at[0], sibling)
    tok_copy.start()
    win_copy = remote(w_in.at[0], win.at[core], one_send.at[1], one_recv.at[1], sibling)
    wout_copy = remote(w_out.at[0], wout.at[core], one_send.at[2], one_recv.at[2], sibling)
    win_copy.start()
    wout_copy.start()

    experts = catalog.shape[1]
    kinds = lax.broadcasted_iota(jnp.int32, (experts, count), 0)
    small_eye = lax.broadcasted_iota(jnp.int32, (experts, experts), 0) == lax.broadcasted_iota(
        jnp.int32, (experts, experts), 1
    )
    slot_column = jnp.sum(
        jnp.where(small_eye, catalog[...].astype(F32), 0.0), axis=1, keepdims=True
    )
    hot = [kinds == routes[k : k + 1, :] for k in range(2)]
    ones = [jnp.where(h, 1.0, 0.0) for h in hot]
    before = (
        lax.broadcasted_iota(jnp.int32, (count, count), 0)
        < lax.broadcasted_iota(jnp.int32, (count, count), 1)
    )
    earlier = jnp.dot(
        (ones[0] + ones[1]).astype(BF16),
        jnp.where(before, 1.0, 0.0).astype(BF16),
        preferred_element_type=F32,
    )
    target = []
    for k in range(2):
        position = jnp.sum(ones[k] * earlier, axis=0, keepdims=True).astype(jnp.int32)
        slot = jnp.sum(ones[k] * slot_column, axis=0, keepdims=True).astype(jnp.int32)
        dz = jnp.bitwise_and((slot >> 1) - z + nz, nz - 1)
        order = jnp.where(dz == 0, 0, jnp.where(2 * dz <= nz, 2 * dz - 1, 2 * (nz - dz)))
        mine = jnp.bitwise_and(slot + xl, 1) == core
        target.append(jnp.where(mine, order * CAP + position, -1))
    every = lax.broadcasted_iota(jnp.int32, (nz * CAP, count), 0)
    pick = jnp.where((every == target[0]) | (every == target[1]), 1.0, 0.0).astype(BF16)

    column = [as_column(t.astype(F32)) for t in target]
    high, low = [], []
    for k in range(2):
        value = fixed[k : k + 1, :]
        high.append(as_column((value >> 8).astype(F32)))
        low.append(as_column(jnp.bitwise_and(value, 255).astype(F32)))
    for k in range(CHUNKS):
        lane = (lax.broadcasted_iota(jnp.int32, (count, rows), 1) + k * rows).astype(F32)
        for ref, part in ((pick_hi, high), (pick_lo, low)):
            ref[k] = (
                jnp.where(lane == column[0], part[0], 0.0)
                + jnp.where(lane == column[1], part[1], 0.0)
            ).astype(BF16)

    def wait_stat(offset, carry):
        stat_copy(offset).wait_recv()
        return carry + stat_in[offset]

    sums = lax.fori_loop(1, PLACES, wait_stat, stat_out[...])
    mean_row = sums[0:1, :] / D
    inverse_row = lax.rsqrt(sums[1:2, :] / D - mean_row * mean_row + 1e-06)
    mean, inverse = as_column(mean_row), as_column(inverse_row)
    remote(tokens, tok2.at[1 - core], one_send.at[0], one_recv.at[0], sibling).wait_recv()
    both = jnp.concatenate([tok2[0], tok2[1]], axis=1).astype(F32)
    lanes = pl.ds(pl.multiple_of(chip * WIDE, WIDE), WIDE)
    normed = ((both - mean) * inverse * (1.0 + scale[:, lanes]) + shift[:, lanes]).astype(BF16)
    sent_rows[...] = to_messages(jnp.dot(pick, normed, preferred_element_type=F32))

    def disp_copy(d):
        return remote(
            sent_rows.at[d], got_rows.at[d], disp_send.at[d], disp_recv.at[d], peer(step_of(d))
        )

    def start_disp(d, carry):
        disp_copy(d).start()
        return carry

    @pl.when(core == 1)
    def _():
        disp_copy(0).start()

    lax.fori_loop(1, nz, start_disp, 0)

    @pl.when(core == 0)
    def _():
        got_rows[0] = sent_rows[0]

    waits = []

    def go(copy):
        copy.start()
        waits.append(copy)

    def wait_disp(d, carry):
        disp_copy(d).wait_recv()
        return carry

    def gather_start(k):
        lo = k * slots_chunk
        if k == 0:
            @pl.when(core == 1)
            def _():
                disp_copy(0).wait_recv()

        lax.fori_loop(max(lo, 1), lo + slots_chunk, wait_disp, 0)
        held[k, chip] = to_rows(got_rows[lo : lo + slots_chunk])
        mine = held.at[k, chip]
        go(remote(mine, mine, gat_send.at[k, 0], gat_recv.at[k, 0], across))
        go(remote(mine, mine, gat_send.at[k, 1], gat_recv.at[k, 1], right))
        go(remote(mine, mine, gat_send.at[k, 2], gat_recv.at[k, 2], left))

    def arrived(k, i, ref):
        remote(ref, ref, gat_send.at[k, i], gat_recv.at[k, i], across).wait_recv()

    def gather_across(k):
        other = held.at[k, piece(y, 0)]
        arrived(k, 0, other)
        go(remote(other, other, gat_send.at[k, 3], gat_recv.at[k, 3], right))
        go(remote(other, other, gat_send.at[k, 4], gat_recv.at[k, 4], left))

    def gather_pass(k, a):
        base = 1 + 2 * (1 - a)
        from_left, from_right = held.at[k, piece(y_left, a)], held.at[k, piece(y_right, a)]
        first, second = pl.ds(0, half), pl.ds(half, half)
        arrived(k, base, from_left)
        ref = from_left.at[first]
        go(remote(ref, ref, gat_send.at[k, base + 4], gat_recv.at[k, base + 4], right))
        arrived(k, base + 1, from_right)
        ref = from_right.at[second]
        go(remote(ref, ref, gat_send.at[k, base + 5], gat_recv.at[k, base + 5], left))

    def gather_end(k, a):
        base = 5 + 2 * (1 - a)
        far = held.at[k, piece(y_far, a)]
        arrived(k, base, far.at[pl.ds(0, half)])
        arrived(k, base + 1, far.at[pl.ds(half, half)])

    tiles = win.shape[2] // WIDE

    def hidden(k):
        x = jnp.concatenate([held[k, q] for q in range(CHIPS)], axis=1)
        for c in range(2):
            for t in range(tiles):
                h = jnp.dot(
                    x, win[c, :, t * WIDE : (t + 1) * WIDE], preferred_element_type=F32
                )
                hid[c, :, t * WIDE : (t + 1) * WIDE] = jax.nn.gelu(h, approximate=True).astype(BF16)

    def second(q):
        lanes_q = pl.ds(pl.multiple_of(q * WIDE, WIDE), WIDE)
        return jnp.dot(hid[0], wout[0, :, lanes_q], preferred_element_type=F32) + jnp.dot(
            hid[1], wout[1, :, lanes_q], preferred_element_type=F32
        )

    def landed(k, i, ref):
        remote(ref, ref, red_send.at[k, i], red_recv.at[k, i], across).wait_recv()

    def reduce_start(k):
        for a in range(2):
            far_out[k, a] = second(piece(y_far, a)).astype(BF16)
            for i, to in ((0, right), (1, left)):
                src = far_out.at[k, a, pl.ds(i * half, half)]
                dst = far_in.at[k, a, pl.ds(i * half, half)]
                go(remote(src, dst, red_send.at[k, 2 * i + a], red_recv.at[k, 2 * i + a], to))
        for a in range(2):
            part_near[a, 0] = second(piece(y_right, a))
            part_near[a, 1] = second(piece(y_left, a))
        for a in range(2):
            part_own[k, a] = second(piece(y, a))

    def reduce_near(k, a):
        for i, to in ((0, right), (1, left)):
            here = pl.ds(i * half, half)
            rest = pl.ds((1 - i) * half, half)
            landed(k, 2 * i + a, far_in.at[k, a, here])
            near_out[k, a, i, here] = (
                part_near[a, i, here] + far_in[k, a, here].astype(F32)
            ).astype(BF16)
            near_out[k, a, i, rest] = part_near[a, i, rest].astype(BF16)
            j = 4 + 2 * i + a
            go(
                remote(
                    near_out.at[k, a, i], near_in.at[k, a, i], red_send.at[k, j], red_recv.at[k, j], to
                )
            )

    def reduce_own(k, a):
        total = part_own[k, a]
        for i in range(2):
            landed(k, 4 + 2 * i + a, near_in.at[k, a, i])
            total = total + near_in[k, a, i].astype(F32)
        return total

    def reduce_across(k):
        x_out[k] = reduce_own(k, 0).astype(BF16)
        go(remote(x_out.at[k], x_in.at[k], red_send.at[k, 8], red_recv.at[k, 8], across))

    def back_copy(d):
        return remote(
            back_out.at[d], back_in.at[d], back_send.at[d], back_recv.at[d], peer(nz - step_of(d))
        )

    def start_back(d, carry):
        back_copy(d).start()
        return carry

    def wait_back(d, carry):
        back_copy(d).wait_recv()
        return carry

    def give_back(k):
        mine = reduce_own(k, 1)
        landed(k, 8, x_in.at[k])
        lo = k * slots_chunk
        back_out[lo : lo + slots_chunk] = to_messages(mine + x_in[k].astype(F32))
        if k == 0:
            @pl.when(core == 1)
            def _():
                back_copy(0).start()

            @pl.when(core == 0)
            def _():
                back_in[0] = back_out[0]

        lax.fori_loop(max(lo, 1), lo + slots_chunk, start_back, 0)

    def combine(k):
        lo = k * slots_chunk
        if k == 0:
            @pl.when(core == 1)
            def _():
                back_copy(0).wait_recv()

        lax.fori_loop(max(lo, 1), lo + slots_chunk, wait_back, 0)
        values = to_rows(back_in[lo : lo + slots_chunk])
        return 256.0 * jnp.dot(pick_hi[k], values, preferred_element_type=F32) + jnp.dot(
            pick_lo[k], values, preferred_element_type=F32
        )

    for k in range(CHUNKS):
        gather_start(k)
    for k in range(CHUNKS):
        gather_across(k)
    for k in range(CHUNKS):
        gather_pass(k, 1)
    for k in range(CHUNKS):
        gather_pass(k, 0)
    load_in.wait()
    load_out.wait()
    remote(w_in.at[0], win.at[1 - core], one_send.at[1], one_recv.at[1], sibling).wait_recv()
    remote(w_out.at[0], wout.at[1 - core], one_send.at[2], one_recv.at[2], sibling).wait_recv()
    for k in range(CHUNKS):
        gather_end(k, 1)
        gather_end(k, 0)
        hidden(k)
        reduce_start(k)
        for a in range(2):
            reduce_near(k, a)
        reduce_across(k)
        give_back(k)
    answer = combine(0)
    for k in range(1, CHUNKS):
        answer = answer + combine(k)
    answer = answer / 65536.0
    comb[0] = answer[:, :LANES]
    comb[1] = answer[:, LANES:]
    comb_copy = remote(comb.at[1 - core], comb_in, one_send.at[3], one_recv.at[3], sibling)
    comb_copy.start()
    comb_copy.wait_recv()
    my_lanes = pl.ds(pl.multiple_of(place * LANES, LANES), LANES)
    out[...] = (
        tokens[...].astype(F32) + gate[:, my_lanes] * (comb[core] + comb_in[...])
    ).astype(BF16)

    comb_copy.wait_send()
    tok_copy.wait_send()
    win_copy.wait_send()
    wout_copy.wait_send()
    for copy in waits:
        copy.wait_send()

    def left_stat(offset, carry):
        stat_copy(offset).wait_send()
        return carry

    def left_rows(d, carry):
        disp_copy(d).wait_send()
        back_copy(d).wait_send()
        return carry

    lax.fori_loop(1, PLACES, left_stat, 0)
    lax.fori_loop(1, nz, left_rows, 0)

    @pl.when(core == 1)
    def _():
        left_rows(0, 0)


def shards(
    tokens, mod_shift, mod_scale, res_gate, weight_in, weight_out, expert_slot, routes, gate_fixed
):
    n_tok = lax.axis_size("tok")
    nz = n_tok // 2
    count = tokens.shape[0]
    units = weight_in.shape[2]
    rows = nz // CHUNKS * CAP
    vmem = pl.BlockSpec(memory_space=pltpu.VMEM)
    anywhere = pl.BlockSpec(memory_space=pl.ANY)
    dma = pltpu.SemaphoreType.DMA
    scratch = [
        pltpu.VMEM((2, count, LANES), BF16),
        pltpu.VMEM((8, count), F32),
        pltpu.VMEM((PLACES, 8, count), F32),
        pltpu.VMEM((nz, 2 * CAP, LANES), BF16),
        pltpu.VMEM((nz, 2 * CAP, LANES), BF16),
        pltpu.VMEM((CHUNKS, CHIPS, rows, WIDE), BF16),
        pltpu.VMEM((2, D, units), BF16),
        pltpu.VMEM((2, units, D), BF16),
        pltpu.VMEM((2, rows, units), BF16),
        pltpu.VMEM((CHUNKS, 2, rows, WIDE), F32),
        pltpu.VMEM((2, 2, rows, WIDE), F32),
        pltpu.VMEM((CHUNKS, 2, rows, WIDE), BF16),
        pltpu.VMEM((CHUNKS, 2, rows, WIDE), BF16),
        pltpu.VMEM((CHUNKS, 2, 2, rows, WIDE), BF16),
        pltpu.VMEM((CHUNKS, 2, 2, rows, WIDE), BF16),
        pltpu.VMEM((CHUNKS, rows, WIDE), BF16),
        pltpu.VMEM((CHUNKS, rows, WIDE), BF16),
        pltpu.VMEM((nz, 2 * CAP, LANES), BF16),
        pltpu.VMEM((nz, 2 * CAP, LANES), BF16),
        pltpu.VMEM((CHUNKS, count, rows), BF16),
        pltpu.VMEM((CHUNKS, count, rows), BF16),
        pltpu.VMEM((2, count, LANES), F32),
        pltpu.VMEM((count, LANES), F32),
        dma((2,)),
        dma((4,)),
        dma((4,)),
        dma((PLACES,)),
        dma((PLACES,)),
        dma((nz,)),
        dma((nz,)),
        dma((CHUNKS, 9)),
        dma((CHUNKS, 9)),
        dma((CHUNKS, 9)),
        dma((CHUNKS, 9)),
        dma((nz,)),
        dma((nz,)),
    ]
    return pl.pallas_call(
        functools.partial(kernel, n_tok),
        out_shape=jax.ShapeDtypeStruct(tokens.shape, BF16),
        in_specs=[vmem] * 7 + [anywhere] * 2,
        out_specs=vmem,
        scratch_shapes=scratch,
        compiler_params=pltpu.CompilerParams(
            collective_id=0, has_side_effects=True, vmem_limit_bytes=48 * 1024 * 1024
        ),
        cost_estimate=pl.CostEstimate(
            flops=4 * 2 * rows * CHUNKS * D * units,
            bytes_accessed=4 * D * units,
            transcendentals=2 * rows * CHUNKS * units,
        ),
    )(
        tokens,
        mod_shift[None, :],
        mod_scale[None, :],
        res_gate[None, :],
        routes.T,
        gate_fixed.T,
        expert_slot[None, :],
        weight_in,
        weight_out,
    )


def solution(mesh):
    placed = (
        P("tok", "place"),
        P(),
        P(),
        P(),
        P("tok", None, "place"),
        P("tok", "place", None),
        P(),
        P("tok", None),
        P("tok", None),
    )
    return jax.shard_map(
        shards, mesh=mesh, in_specs=placed, out_specs=P("tok", "place"), check_vma=False
    )
```

time: 549 us -> 94.3 us (0.17)
  blocking collectives: 304 us -> 0 us
  waiting for transfers between devices: 153 us -> 0 us
  Pallas kernels: 0 us -> 85.1 us
  local copies, waits for them, and re-layouts: 59.7 us -> 8.76 us
  between operations: 13.5 us -> 0.02 us
  other arithmetic: 9.68 us -> 0 us
  matrix products: 7.99 us -> 0 us
    all_to_all x2 -> x0, blocking collectives: 304 us -> none  [the longest x1 156 us: shards(): lax.all_to_all(outgoing, 'tok', split_axis=0, concat_axis=0, tiled=True)]
    unnamed x3 -> x0, waiting for transfers between devices: 90.2 us -> none
    pallas_call x0 -> x1, Pallas kernels: none -> 85.1 us  [shards(): pl.pallas_call(functools.partial(kernel, n_tok), out_shape=jax.ShapeDtype...]
    all_gather x1 -> x0, waiting for transfers between devices: 62.7 us -> none  [shards(): lax.all_gather(tokens, 'place', axis=1, tiled=True).astype(jnp.float32)]
    unnamed x11 -> x19, local copies, waits for them, and re-layouts: 52.7 us -> 8.76 us
    dot_general x1 -> x0, matrix products: 7.99 us -> none  [shards(): jnp.einsum('nscf,sfd->nscd', activated, weight_out, preferred_element_typ...]
    gather x2 -> x0, local copies, waits for them, and re-layouts: 5.61 us -> none  [the longest x1 4.27 us: shards(): normed[token_index]]
  transfers between devices with their start and end apart: 2 -> 0, of which waited for: 2 -> 0; matrix products, arithmetic and copies ran while one was open for 1% -> 0% of each run, Pallas kernels for 0% -> 0%
where the time goes in v1:
time: 94.3 us; the launch traced here: 93.9 us
  Pallas kernels  85.1 us (90%)
  local copies, waits for them, and re-layouts  8.76 us (9%)
    pallas_call x1, Pallas kernels, shards(): pl.pallas_call(functools.partial(kernel, n_tok), out_shape=jax.ShapeDtype...  85.1 us
    unnamed x19, local copies, waits for them, and re-layouts  8.76 us

profile of v1, /device:TPU:1, one launch (start us, length us, event | category | flops | bytes accessed | tf_op | source)
XLA Modules:
  0.0 93.9 jit_solution(13225663009290874438)
XLA Ops:
  0.0 0.0 copy-start
  0.0 1.6 %copy-done = bf16[1,2048,512]{2,1,0:T(8,128)(2,1)S(1)} copy-done((bf16[1,2048,512]{2,1,0:T(8,128)(2,1)S(1)}, bf16[1,2048,512]{2,1,0:T(8,128)(2,1)}, u32[]{:S(2)}) %copy-start) | copy-done | bytes 2097176
  1.6 0.0 copy-start.1
  1.6 1.6 %copy-done.1 = bf16[1,512,2048]{2,1,0:T(8,128)(2,1)S(1)} copy-done((bf16[1,512,2048]{2,1,0:T(8,128)(2,1)S(1)}, bf16[1,512,2048]{2,1,0:T(8,128)(2,1)}, u32[]{:S(2)}) %copy-start.1) | copy-done | bytes 2097176
  3.2 0.0 copy-start.2
  3.2 0.8 copy-done.2
  4.0 0.0 copy-start.3
  4.0 0.7 copy-done.3
  4.7 0.0 copy-start.4
  4.7 0.7 copy-done.4
  5.4 0.0 copy-start.5
  5.4 0.7 copy-done.5
  6.1 0.0 copy-start.6
  6.1 0.7 copy-done.6
  6.8 0.0 copy-start.7
  6.8 0.7 copy-done.7
  7.5 0.0 copy-start.8
  7.5 0.7 copy-done.8
  8.1 85.1 %shard_map.91 = bf16[256,128]{1,0:T(8,128)(2,1)S(1)} custom-call(bf16[256,128]{1,0:T(8,128)(2,1)S(1)} %copy-done.2, f32[1,2048]{1,0:T(1,128)S(1)} %bitcast.6, f32[1,2048]{1,0:T(1,128)S(1)} %bitcast.7, f32[1,2048]{1,0:T(1,128)S(1)} %bitcast.8, s32[2,256]{1,0:T(2,128)S(1)} %bitcast.9, s32[2,256]{1,0:T(2,128)S(1)} %bitcast.10, s32[1,32]{1,0:T(1,128)S(1)} %bitcast.11, ...), custom_call_target="tpu_custom_call" | custom-call | flops 3221225472 | bytes 4194304 | tf_op jit(solution)/shard_map/pallas_call | solution.py:517
  93.3 0.6 copy.11
Async XLA Ops:
  0.0 1.6 %copy-start = (bf16[1,2048,512]{2,1,0:T(8,128)(2,1)S(1)}, bf16[1,2048,512]{2,1,0:T(8,128)(2,1)}, u32[]{:S(2)}) copy-start(bf16[1,2048,512]{2,1,0:T(8,128)(2,1)} %w_in.1) | copy-start | bytes 6291460
  1.6 1.6 %copy-start.1 = (bf16[1,512,2048]{2,1,0:T(8,128)(2,1)S(1)}, bf16[1,512,2048]{2,1,0:T(8,128)(2,1)}, u32[]{:S(2)}) copy-start(bf16[1,512,2048]{2,1,0:T(8,128)(2,1)} %w_out.1) | copy-start | bytes 6291460
  3.2 0.8 copy-start.2
  4.0 0.7 copy-start.3
  4.7 0.7 copy-start.4
  5.4 0.7 copy-start.5
  6.1 0.7 copy-start.6
  6.8 0.7 copy-start.7
  7.5 0.7 copy-start.8

commit v2 on v0

v2 whole, which is shorter than its diff:
```python
import functools

import jax
import jax.numpy as jnp
from jax import lax
from jax.experimental import pallas as pl
from jax.experimental.pallas import tpu as pltpu
from jax.sharding import PartitionSpec as P

D = 2048
CAP = 24
CHUNKS = 4
STEPS = (0, 1, 15, 2, 14, 3, 13, 4, 12, 5, 11, 6, 10, 7, 9, 8)
GATHER = "DBDD"
REDUCE = "ADDD"
ORDER = (
    ("A", 0), ("A", 1), ("A", 2), ("H", 0), ("F1L", 1), ("F1R", 1), ("A", 3), ("S0", 0), ("S1", 0),
    ("SN", 0), ("SO", 0), ("H", 2), ("G", 1), ("S", 2), ("SO", 2), ("N0R", 0), ("N0L", 0), ("N1R", 0),
    ("N1L", 0), ("H", 3), ("S", 3), ("SO", 3), ("H", 1), ("S", 1), ("O0", 0), ("SO", 1), ("O1", 2),
    ("O1", 3), ("C", 2), ("O1", 1), ("O1", 0), ("C", 3), ("C", 1), ("C", 0),
)
CHIPS = 8
PLACES = 16
LANES = 128
WIDE = 256
MESH = pl.DeviceIdType.MESH
F32 = jnp.float32
BF16 = jnp.bfloat16


def remote(src, dst, send_sem, recv_sem, device):
    return pltpu.make_async_remote_copy(
        src_ref=src,
        dst_ref=dst,
        send_sem=send_sem,
        recv_sem=recv_sem,
        device_id=device,
        device_id_type=MESH,
    )


def to_rows(block):
    slots = block.shape[0]
    wide = block.astype(F32)
    halves = [wide[:, h * CAP : (h + 1) * CAP].reshape(slots * CAP, LANES) for h in range(2)]
    return jnp.concatenate(halves, axis=1).astype(BF16)


def to_messages(rows):
    slots = rows.shape[0] // CAP
    halves = [rows[:, h * LANES : (h + 1) * LANES].reshape(slots, CAP, LANES) for h in range(2)]
    return jnp.concatenate(halves, axis=1).astype(BF16)


def kernel(
    n_tok,
    tokens_hbm,
    shift_hbm,
    scale_hbm,
    gate_hbm,
    routes_hbm,
    fixed_hbm,
    catalog_hbm,
    w_in,
    w_out,
    out,
    shift,
    scale,
    gate,
    routes,
    fixed,
    catalog,
    tok2,
    sent_rows,
    got_rows,
    held,
    normed,
    win,
    wout,
    hid,
    part_own,
    part_near,
    far_out,
    far_in,
    near_out,
    near_in,
    x_out,
    x_in,
    back_out,
    back_in,
    pick_hi,
    pick_lo,
    total,
    comb,
    comb_in,
    w_sem,
    one_send,
    one_recv,
    disp_send,
    disp_recv,
    gat_send,
    gat_recv,
    red_send,
    red_recv,
    back_send,
    back_recv,
):
    place, tok = lax.axis_index("place"), lax.axis_index("tok")
    nz = n_tok // 2
    steps = STEPS[:nz]
    slots_chunk = nz // CHUNKS
    rows = slots_chunk * CAP
    half = rows // 2
    first, second = pl.ds(0, half), pl.ds(half, half)
    core, chip = lax.rem(place, 2), lax.div(place, 2)
    xh, y = lax.rem(chip, 2), lax.div(chip, 2)
    z, xl = lax.div(tok, 2), lax.rem(tok, 2)
    sibling = (place + 1 - 2 * core, tok)
    across = (place + 2 - 4 * xh, tok)
    y_right, y_left, y_far = lax.rem(y + 1, 4), lax.rem(y + 3, 4), lax.rem(y + 2, 4)
    right = (y_right * 4 + xh * 2 + core, tok)
    left = (y_left * 4 + xh * 2 + core, tok)

    def mate(offset):
        return (lax.rem(place + 2 * offset, PLACES), tok)

    def peer(dz):
        return (place, lax.rem(z + dz, nz) * 2 + lax.rem(xl + core, 2))

    def piece(y_of, a):
        return y_of * 2 + lax.rem(xh + 1 + a, 2)

    barrier = pltpu.get_barrier_semaphore()

    def greet(device):
        pl.semaphore_signal(barrier, inc=1, device_id=device, device_id_type=MESH)

    for dz in steps[1:]:
        greet(peer(dz))

    @pl.when(core == 1)
    def _():
        greet(peer(0))

    for offset in range(1, CHIPS):
        greet(mate(offset))
    greet(sibling)

    lanes = pl.ds(pl.multiple_of(chip * WIDE, WIDE), WIDE)
    my_lanes = pl.ds(pl.multiple_of(place * LANES, LANES), LANES)
    pairs = (
        (routes_hbm, routes),
        (catalog_hbm, catalog),
        (tokens_hbm, tok2.at[core]),
        (fixed_hbm, fixed),
        (scale_hbm, scale),
        (shift_hbm, shift),
        (gate_hbm.at[:, my_lanes], gate),
        (w_in.at[0], win.at[core]),
        (w_out.at[0], wout.at[core]),
    )
    loads = [pltpu.make_async_copy(src, dst, w_sem.at[i]) for i, (src, dst) in enumerate(pairs)]
    for copy in loads:
        copy.start()

    loads[0].wait()
    loads[1].wait()
    count = tokens_hbm.shape[0]
    experts = catalog.shape[1]
    kinds = lax.broadcasted_iota(jnp.int32, (experts, count), 0)
    small_eye = lax.broadcasted_iota(jnp.int32, (experts, experts), 0) == lax.broadcasted_iota(
        jnp.int32, (experts, experts), 1
    )
    slot_column = jnp.sum(
        jnp.where(small_eye, catalog[...].astype(F32), 0.0), axis=1, keepdims=True
    )
    ones = [jnp.where(kinds == routes[k : k + 1, :], 1.0, 0.0) for k in range(2)]
    down = lax.broadcasted_iota(jnp.int32, (count, count), 0)
    along = lax.broadcasted_iota(jnp.int32, (count, count), 1)
    earlier = jnp.dot(
        (ones[0] + ones[1]).astype(BF16),
        jnp.where(down < along, 1.0, 0.0).astype(BF16),
        preferred_element_type=F32,
    )
    target = []
    for k in range(2):
        position = jnp.sum(ones[k] * earlier, axis=0, keepdims=True).astype(jnp.int32)
        slot = jnp.sum(ones[k] * slot_column, axis=0, keepdims=True).astype(jnp.int32)
        dz = jnp.bitwise_and((slot >> 1) - z + nz, nz - 1)
        order = jnp.zeros_like(dz)
        for d, step in enumerate(steps):
            order = jnp.where(dz == step, d, order)
        mine = jnp.bitwise_and(slot + xl, 1) == core
        target.append(jnp.where(mine, order * CAP + position, -1))
    every = lax.broadcasted_iota(jnp.int32, (nz * CAP, count), 0)
    pick = jnp.where((every == target[0]) | (every == target[1]), 1.0, 0.0).astype(BF16)

    pl.semaphore_wait(barrier, CHIPS + nz - 1 + core)
    tok_copy = remote(tokens_hbm, tok2.at[core], one_send.at[0], one_recv.at[0], sibling)
    win_copy = remote(w_in.at[0], win.at[core], one_send.at[1], one_recv.at[1], sibling)
    wout_copy = remote(w_out.at[0], wout.at[core], one_send.at[2], one_recv.at[2], sibling)
    tok_copy.start()
    loads[2].wait()
    remote(tokens_hbm, tok2.at[1 - core], one_send.at[0], one_recv.at[0], sibling).wait_recv()

    picked = jnp.dot(
        pick, jnp.concatenate([tok2[0], tok2[1]], axis=1), preferred_element_type=F32
    )
    sent_rows[...] = to_messages(picked)

    def disp_copy(d):
        return remote(
            sent_rows.at[d], got_rows.at[d], disp_send.at[d], disp_recv.at[d], peer(steps[d])
        )

    @pl.when(core == 1)
    def _():
        disp_copy(0).start()

    for d in range(1, nz):
        disp_copy(d).start()

    @pl.when(core == 0)
    def _():
        got_rows[0] = sent_rows[0]

    win_copy.start()
    wout_copy.start()
    for i in range(3, 7):
        loads[i].wait()

    def as_column(row):
        return jnp.sum(jnp.where(down == along, row, 0.0), axis=1, keepdims=True)

    column = [as_column(t.astype(F32)) for t in target]
    high, low = [], []
    for k in range(2):
        value = fixed[k : k + 1, :]
        high.append(as_column((value >> 8).astype(F32)))
        low.append(as_column(jnp.bitwise_and(value, 255).astype(F32)))
    for k in range(CHUNKS):
        lane = (lax.broadcasted_iota(jnp.int32, (count, rows), 1) + k * rows).astype(F32)
        for ref, part in ((pick_hi, high), (pick_lo, low)):
            ref[k] = (
                jnp.where(lane == column[0], part[0], 0.0)
                + jnp.where(lane == column[1], part[1], 0.0)
            ).astype(BF16)

    sends = []

    def gat(k, i, ref, to):
        copy = remote(ref, ref, gat_send.at[k, i], gat_recv.at[k, i], to)
        copy.start()
        sends.append(copy)

    def gat_wait(k, i, ref):
        remote(ref, ref, gat_send.at[k, i], gat_recv.at[k, i], across).wait_recv()

    def red(k, i, src, dst, to):
        copy = remote(src, dst, red_send.at[k, i], red_recv.at[k, i], to)
        copy.start()
        sends.append(copy)

    def red_wait(k, i, ref):
        remote(ref, ref, red_send.at[k, i], red_recv.at[k, i], across).wait_recv()

    def slots_of(k, act):
        for d in range(k * slots_chunk, (k + 1) * slots_chunk):
            if d == 0:
                pl.when(core == 1)(functools.partial(act, d))
            else:
                act(d)

    def arrive(k):
        slots_of(k, lambda d: disp_copy(d).wait_recv())
        held[k, chip] = to_rows(got_rows[k * slots_chunk : (k + 1) * slots_chunk])
        mine = held.at[k, chip]
        if GATHER[k] == "D":
            for offset in DIRECT:
                gat(k, offset - 1, mine, mate(offset))
        else:
            gat(k, 0, mine, across)
            gat(k, 1, mine, right)
            gat(k, 2, mine, left)

    def arrive_across(k):
        other = held.at[k, piece(y, 0)]
        gat_wait(k, 0, other)
        gat(k, 3, other, right)
        gat(k, 4, other, left)

    def pass_on(k, a, from_left):
        i = 1 + 2 * (1 - a) + (0 if from_left else 1)
        ref = held.at[k, piece(y_left if from_left else y_right, a)]
        gat_wait(k, i, ref)
        gat(k, i + 4, ref.at[first if from_left else second], right if from_left else left)
        if GATHER[k] == "B":
            gat(k, i + 2, ref, across)

    def far_across(k):
        far = held.at[k, piece(y_far, 1)]
        gat_wait(k, 5, far.at[first])
        gat_wait(k, 6, far.at[second])
        gat(k, 7, far, across)

    def all_there(k):
        if GATHER[k] == "D":
            for offset in range(1, CHIPS):
                gat_wait(k, offset - 1, held.at[k, lax.rem(chip + CHIPS - offset, CHIPS)])
        elif GATHER[k] == "B":
            gat_wait(k, 0, held.at[k, piece(y, 0)])
            gat_wait(k, 3, held.at[k, piece(y_left, 0)])
            gat_wait(k, 4, held.at[k, piece(y_right, 0)])
            gat_wait(k, 7, held.at[k, piece(y_far, 0)])
        else:
            for a in range(2):
                far = held.at[k, piece(y_far, a)]
                gat_wait(k, 7 - 2 * a, far.at[first])
                gat_wait(k, 8 - 2 * a, far.at[second])

    tiles = win.shape[2] // WIDE
    ready = []

    def hidden(k):
        all_there(k)
        sums = jnp.zeros((rows, WIDE), F32)
        squares = jnp.zeros((rows, WIDE), F32)
        for q in range(CHIPS):
            x = held[k, q].astype(F32)
            sums += x
            squares += x * x
        mean = jnp.sum(sums, axis=1, keepdims=True) / D
        inverse = lax.rsqrt(jnp.sum(squares, axis=1, keepdims=True) / D - mean * mean + 1e-06)
        for q in range(CHIPS):
            at = slice(q * WIDE, (q + 1) * WIDE)
            x = held[k, q].astype(F32)
            normed[:, at] = (
                (x - mean) * inverse * (1.0 + scale[:, at]) + shift[:, at]
            ).astype(BF16)
        if not ready:
            ready.append(k)
            loads[7].wait()
            loads[8].wait()
            for i, (src, dst) in ((1, (w_in, win)), (2, (w_out, wout))):
                remote(src.at[0], dst.at[1 - core], one_send.at[i], one_recv.at[i], sibling).wait_recv()
        for c in range(2):
            for t in range(tiles):
                at = slice(t * WIDE, (t + 1) * WIDE)
                h = jnp.dot(normed[...], win[c, :, at], preferred_element_type=F32)
                hid[c, :, at] = jax.nn.gelu(h, approximate=True).astype(BF16)

    def result(q):
        at = pl.ds(pl.multiple_of(q * WIDE, WIDE), WIDE)
        return jnp.dot(hid[0], wout[0, :, at], preferred_element_type=F32) + jnp.dot(
            hid[1], wout[1, :, at], preferred_element_type=F32
        )

    def far_results(k, a):
        far_out[k, a] = result(piece(y_far, a)).astype(BF16)
        for i, (part, to) in enumerate(((first, right), (second, left))):
            red(k, 2 * i + a, far_out.at[k, a, part], far_in.at[k, a, part], to)

    def near_results(k):
        for a in range(2):
            part_near[a, 0] = result(piece(y_right, a))
            part_near[a, 1] = result(piece(y_left, a))

    def own_results(k):
        if REDUCE[k] == "D":
            part_own[k, 1] = result(chip)
        else:
            for a in range(2):
                part_own[k, a] = result(piece(y, a))

    def near_sum(k, a, i):
        here, rest = (first, second) if i == 0 else (second, first)
        red_wait(k, 2 * i + a, far_in.at[k, a, here])
        near_out[k, a, i, here] = (
            part_near[a, i, here] + far_in[k, a, here].astype(F32)
        ).astype(BF16)
        near_out[k, a, i, rest] = part_near[a, i, rest].astype(BF16)
        j = 4 + 2 * i + a
        red(k, j, near_out.at[k, a, i], near_in.at[k, a, i], right if i == 0 else left)

    def own_sum(k, a):
        value = part_own[k, a]
        for i in range(2):
            red_wait(k, 4 + 2 * i + a, near_in.at[k, a, i])
            value = value + near_in[k, a, i].astype(F32)
        return value

    def sum_across(k):
        x_out[k] = own_sum(k, 0).astype(BF16)
        red(k, 8, x_out.at[k], x_in.at[k], across)

    def block_of(k, i, far, near, x):
        if i < 2:
            return far.at[k, i]
        return near.at[k, (i - 2) // 2, (i - 2) % 2] if i < 6 else x.at[k]

    def direct_results(k):
        for offset in DIRECT:
            src = block_of(k, offset - 1, far_out, near_out, x_out)
            dst = block_of(k, offset - 1, far_in, near_in, x_in)
            src[...] = result(lax.rem(chip + offset, CHIPS)).astype(BF16)
            red(k, offset - 1, src, dst, mate(offset))

    def back_copy(d):
        return remote(
            back_out.at[d], back_in.at[d], back_send.at[d], back_recv.at[d], peer(nz - steps[d])
        )

    def give_back(k):
        if REDUCE[k] == "D":
            value = part_own[k, 1]
            for i in range(CHIPS - 1):
                ref = block_of(k, i, far_in, near_in, x_in)
                red_wait(k, i, ref)
                value = value + ref[...].astype(F32)
        else:
            value = own_sum(k, 1)
            red_wait(k, 8, x_in.at[k])
            value = value + x_in[k].astype(F32)
        back_out[k * slots_chunk : (k + 1) * slots_chunk] = to_messages(value)
        slots_of(k, lambda d: back_copy(d).start())
        if k == 0:
            @pl.when(core == 0)
            def _():
                back_in[0] = back_out[0]

    begun = []

    def combine(k):
        slots_of(k, lambda d: back_copy(d).wait_recv())
        values = to_rows(back_in[k * slots_chunk : (k + 1) * slots_chunk])
        part = 256.0 * jnp.dot(pick_hi[k], values, preferred_element_type=F32) + jnp.dot(
            pick_lo[k], values, preferred_element_type=F32
        )
        total[...] = total[...] + part if begun else part
        begun.append(k)

    tasks = {
        "A": arrive,
        "X": arrive_across,
        "F1L": lambda k: pass_on(k, 1, True),
        "F1R": lambda k: pass_on(k, 1, False),
        "F0L": lambda k: pass_on(k, 0, True),
        "F0R": lambda k: pass_on(k, 0, False),
        "G": far_across,
        "H": hidden,
        "S0": lambda k: far_results(k, 0),
        "S1": lambda k: far_results(k, 1),
        "SN": near_results,
        "SO": own_results,
        "N0R": lambda k: near_sum(k, 0, 0),
        "N0L": lambda k: near_sum(k, 0, 1),
        "N1R": lambda k: near_sum(k, 1, 0),
        "N1L": lambda k: near_sum(k, 1, 1),
        "O0": sum_across,
        "S": direct_results,
        "O1": give_back,
        "C": combine,
    }
    for name, k in ORDER:
        tasks[name](k)

    answer = total[...] / 65536.0
    comb[0] = answer[:, :LANES]
    comb[1] = answer[:, LANES:]
    comb_copy = remote(comb.at[1 - core], comb_in, one_send.at[3], one_recv.at[3], sibling)
    comb_copy.start()
    for copy in [tok_copy, win_copy, wout_copy] + sends:
        copy.wait_send()
    for k in range(CHUNKS):
        slots_of(k, lambda d: disp_copy(d).wait_send())
        slots_of(k, lambda d: back_copy(d).wait_send())
    comb_copy.wait_recv()
    out[...] = (tok2[core].astype(F32) + gate[...] * (comb[core] + comb_in[...])).astype(BF16)
    comb_copy.wait_send()


DIRECT = (2, 6, 1, 7, 3, 5, 4)


def shards(
    tokens, mod_shift, mod_scale, res_gate, weight_in, weight_out, expert_slot, routes, gate_fixed
):
    n_tok = lax.axis_size("tok")
    nz = n_tok // 2
    count = tokens.shape[0]
    units = weight_in.shape[2]
    rows = nz // CHUNKS * CAP
    hbm = pl.BlockSpec(memory_space=pltpu.HBM)
    dma = pltpu.SemaphoreType.DMA
    scratch = [
        pltpu.VMEM((1, D), F32),
        pltpu.VMEM((1, D), F32),
        pltpu.VMEM((1, LANES), F32),
        pltpu.VMEM((2, count), jnp.int32),
        pltpu.VMEM((2, count), jnp.int32),
        pltpu.VMEM((1, n_tok), jnp.int32),
        pltpu.VMEM((2, count, LANES), BF16),
        pltpu.VMEM((nz, 2 * CAP, LANES), BF16),
        pltpu.VMEM((nz, 2 * CAP, LANES), BF16),
        pltpu.VMEM((CHUNKS, CHIPS, rows, WIDE), BF16),
        pltpu.VMEM((rows, D), BF16),
        pltpu.VMEM((2, D, units), BF16),
        pltpu.VMEM((2, units, D), BF16),
        pltpu.VMEM((2, rows, units), BF16),
        pltpu.VMEM((CHUNKS, 2, rows, WIDE), F32),
        pltpu.VMEM((2, 2, rows, WIDE), F32),
        pltpu.VMEM((CHUNKS, 2, rows, WIDE), BF16),
        pltpu.VMEM((CHUNKS, 2, rows, WIDE), BF16),
        pltpu.VMEM((CHUNKS, 2, 2, rows, WIDE), BF16),
        pltpu.VMEM((CHUNKS, 2, 2, rows, WIDE), BF16),
        pltpu.VMEM((CHUNKS, rows, WIDE), BF16),
        pltpu.VMEM((CHUNKS, rows, WIDE), BF16),
        pltpu.VMEM((nz, 2 * CAP, LANES), BF16),
        pltpu.VMEM((nz, 2 * CAP, LANES), BF16),
        pltpu.VMEM((CHUNKS, count, rows), BF16),
        pltpu.VMEM((CHUNKS, count, rows), BF16),
        pltpu.VMEM((count, WIDE), F32),
        pltpu.VMEM((2, count, LANES), F32),
        pltpu.VMEM((count, LANES), F32),
        dma((9,)),
        dma((4,)),
        dma((4,)),
        dma((nz,)),
        dma((nz,)),
        dma((CHUNKS, 9)),
        dma((CHUNKS, 9)),
        dma((CHUNKS, 9)),
        dma((CHUNKS, 9)),
        dma((nz,)),
        dma((nz,)),
    ]
    return pl.pallas_call(
        functools.partial(kernel, n_tok),
        out_shape=jax.ShapeDtypeStruct(tokens.shape, BF16),
        in_specs=[hbm] * 9,
        out_specs=pl.BlockSpec(memory_space=pltpu.VMEM),
        scratch_shapes=scratch,
        compiler_params=pltpu.CompilerParams(
            collective_id=0, has_side_effects=True, vmem_limit_bytes=60 * 1024 * 1024
        ),
        cost_estimate=pl.CostEstimate(
            flops=4 * 2 * rows * CHUNKS * D * units,
            bytes_accessed=4 * D * units,
            transcendentals=2 * rows * CHUNKS * units,
        ),
    )(
        tokens,
        mod_shift[None, :],
        mod_scale[None, :],
        res_gate[None, :],
        routes.T,
        gate_fixed.T,
        expert_slot[None, :],
        weight_in,
        weight_out,
    )


def solution(mesh):
    placed = (
        P("tok", "place"),
        P(),
        P(),
        P(),
        P("tok", None, "place"),
        P("tok", "place", None),
        P(),
        P("tok", None),
        P("tok", None),
    )
    return jax.shard_map(
        shards, mesh=mesh, in_specs=placed, out_specs=P("tok", "place"), check_vma=False
    )
```

time: 549 us -> 71.3 us (0.13)
  blocking collectives: 304 us -> 0 us
  waiting for transfers between devices: 153 us -> 0 us
  Pallas kernels: 0 us -> 69.7 us
  local copies, waits for them, and re-layouts: 59.7 us -> 1.47 us
  between operations: 13.5 us -> 0.01 us
  other arithmetic: 9.68 us -> 0 us
  matrix products: 7.99 us -> 0 us
    all_to_all x2 -> x0, blocking collectives: 304 us -> none  [the longest x1 156 us: shards(): lax.all_to_all(outgoing, 'tok', split_axis=0, concat_axis=0, tiled=True)]
    unnamed x3 -> x0, waiting for transfers between devices: 90.2 us -> none
    pallas_call x0 -> x1, Pallas kernels: none -> 69.7 us  [shards(): pl.pallas_call(functools.partial(kernel, n_tok), out_shape=jax.ShapeDtype...]
    all_gather x1 -> x0, waiting for transfers between devices: 62.7 us -> none  [shards(): lax.all_gather(tokens, 'place', axis=1, tiled=True).astype(jnp.float32)]
    unnamed x11 -> x1, local copies, waits for them, and re-layouts: 52.7 us -> 1.47 us
    dot_general x1 -> x0, matrix products: 7.99 us -> none  [shards(): jnp.einsum('nscf,sfd->nscd', activated, weight_out, preferred_element_typ...]
    gather x2 -> x0, local copies, waits for them, and re-layouts: 5.61 us -> none  [the longest x1 4.27 us: shards(): normed[token_index]]
  transfers between devices with their start and end apart: 2 -> 0, of which waited for: 2 -> 0; matrix products, arithmetic and copies ran while one was open for 1% -> 0% of each run, Pallas kernels for 0% -> 0%
where the time goes in v2:
time: 71.3 us; the launch traced here: 71.1 us
  Pallas kernels  69.7 us (98%)
  local copies, waits for them, and re-layouts  1.47 us (2%)
    pallas_call x1, Pallas kernels, shards(): pl.pallas_call(functools.partial(kernel, n_tok), out_shape=jax.ShapeDtype...  69.7 us
    unnamed x1, local copies, waits for them, and re-layouts  1.47 us

profile of v2, /device:TPU:1, one launch (start us, length us, event | category | flops | bytes accessed | tf_op | source)
XLA Modules:
  0.0 71.1 jit_solution(14393931087702014026)
XLA Ops:
  0.0 69.7 %shard_map.91 = bf16[256,128]{1,0:T(8,128)(2,1)} custom-call(bf16[256,128]{1,0:T(8,128)(2,1)} %tokens_hbm.1, f32[1,2048]{1,0:T(1,128)} %bitcast.6, f32[1,2048]{1,0:T(1,128)} %bitcast.7, f32[1,2048]{1,0:T(1,128)} %bitcast.8, s32[2,256]{1,0:T(2,128)} %bitcast.9, s32[2,256]{1,0:T(2,128)} %bitcast.10, s32[1,32]{1,0:T(1,128)} %bitcast.11, ...), custom_call_target="tpu_custom_call" | custom-call | flops 3221225472 | bytes 4194304 | tf_op jit(solution)/shard_map/pallas_call | solution.py:537
  69.7 1.5 %copy.11 = bf16[256,128]{1,0:T(8,128)(2,1)} copy(bf16[256,128]{1,0:T(8,128)(2,1)} %shard_map.91) | data formatting | bytes 131072

commit v3 on v2

--- a/solution.py
+++ b/solution.py
@@ -9,15 +9,17 @@
 
 D = 2048
 CAP = 24
-CHUNKS = 4
-STEPS = (0, 1, 15, 2, 14, 3, 13, 4, 12, 5, 11, 6, 10, 7, 9, 8)
+STEPS = (0, 14, 1, 15, 4, 13, 3, 2, 8, 11, 6, 5, 12, 7, 9, 10)
+SIZES = (4, 4, 4, 4)
+SENDS = (0, 2, 1, 3)
+CHUNKS = len(SIZES)
 GATHER = "DBDD"
 REDUCE = "ADDD"
 ORDER = (
-    ("A", 0), ("A", 1), ("A", 2), ("H", 0), ("F1L", 1), ("F1R", 1), ("A", 3), ("S0", 0), ("S1", 0),
-    ("SN", 0), ("SO", 0), ("H", 2), ("G", 1), ("S", 2), ("SO", 2), ("N0R", 0), ("N0L", 0), ("N1R", 0),
-    ("N1L", 0), ("H", 3), ("S", 3), ("SO", 3), ("H", 1), ("S", 1), ("O0", 0), ("SO", 1), ("O1", 2),
-    ("O1", 3), ("C", 2), ("O1", 1), ("O1", 0), ("C", 3), ("C", 1), ("C", 0),
+    ("A", 0), ("A", 2), ("A", 1), ("H", 0), ("A", 3), ("S0", 0), ("S1", 0), ("SN", 0), ("SO", 0), ("H", 2),
+    ("F1L", 1), ("F1R", 1), ("S", 2), ("SO", 2), ("N0R", 0), ("N0L", 0), ("H", 3), ("G", 1), ("N1R", 0),
+    ("N1L", 0), ("S", 3), ("SO", 3), ("O0", 0), ("O1", 2), ("H", 1), ("S", 1), ("SO", 1), ("O1", 3),
+    ("O1", 0), ("C", 2), ("O1", 1), ("C", 0), ("C", 3), ("C", 1),
 )
 CHIPS = 8
 PLACES = 16
@@ -37,6 +39,10 @@
         device_id=device,
         device_id_type=MESH,
     )
+
+
+def lane_of(kinds, k, i):
+    return sum(1 if kind == "D" else 9 for kind in kinds[:k]) + (0 if kinds[k : k + 1] == "D" else i)
 
 
 def to_rows(block):
@@ -86,6 +92,8 @@
     near_in,
     x_out,
     x_in,
+    all_out,
+    all_in,
     back_out,
     back_in,
     pick_hi,
@@ -107,11 +115,14 @@
 ):
     place, tok = lax.axis_index("place"), lax.axis_index("tok")
     nz = n_tok // 2
-    steps = STEPS[:nz]
-    slots_chunk = nz // CHUNKS
-    rows = slots_chunk * CAP
-    half = rows // 2
-    first, second = pl.ds(0, half), pl.ds(half, half)
+    steps = STEPS
+    starts = [sum(SIZES[:k]) for k in range(CHUNKS)]
+    spans = [slice(start, start + size) for start, size in zip(starts, SIZES)]
+    counts = [size * CAP for size in SIZES]
+    whole = [pl.ds(0, rows) for rows in counts]
+    first = (slice(None), pl.ds(0, LANES))
+    second = (slice(None), pl.ds(LANES, LANES))
+    home = steps.index(0)
     core, chip = lax.rem(place, 2), lax.div(place, 2)
     xh, y = lax.rem(chip, 2), lax.div(chip, 2)
     z, xl = lax.div(tok, 2), lax.rem(tok, 2)
@@ -121,8 +132,25 @@
     right = (y_right * 4 + xh * 2 + core, tok)
     left = (y_left * 4 + xh * 2 + core, tok)
 
-    def mate(offset):
-        return (lax.rem(place + 2 * offset, PLACES), tok)
+    def chip_at(dy, dx):
+        return lax.rem(y + dy, 4) * 2 + lax.rem(xh + dx, 2)
+
+    def chunk_of(d):
+        return max(k for k in range(CHUNKS) if starts[k] <= d)
+
+    def per_chunk(k, act):
+        if starts[k] == home:
+            pl.when(core == 1)(lambda: act(pl.ds(home, SIZES[k])))
+            if SIZES[k] > 1:
+                pl.when(core == 0)(lambda: act(pl.ds(home + 1, SIZES[k] - 1)))
+        else:
+            act(pl.ds(starts[k], SIZES[k]))
+
+    def took(sem, ref):
+        remote(ref, ref, sem, sem, across).wait_recv()
+
+    def mate(dy, dx):
+        return (chip_at(dy, dx) * 2 + core, tok)
 
     def peer(dz):
         return (place, lax.rem(z + dz, nz) * 2 + lax.rem(xl + core, 2))
@@ -135,15 +163,16 @@
     def greet(device):
         pl.semaphore_signal(barrier, inc=1, device_id=device, device_id_type=MESH)
 
-    for dz in steps[1:]:
-        greet(peer(dz))
+    for dz in sorted(steps, key=lambda dz: -min(dz, nz - dz)):
+        if dz:
+            greet(peer(dz))
 
     @pl.when(core == 1)
     def _():
         greet(peer(0))
 
-    for offset in range(1, CHIPS):
-        greet(mate(offset))
+    for dy, dx in DIRECT:
+        greet(mate(dy, dx))
     greet(sibling)
 
     lanes = pl.ds(pl.multiple_of(chip * WIDE, WIDE), WIDE)
@@ -209,20 +238,24 @@
     sent_rows[...] = to_messages(picked)
 
     def disp_copy(d):
+        at = chunk_of(d)
         return remote(
-            sent_rows.at[d], got_rows.at[d], disp_send.at[d], disp_recv.at[d], peer(steps[d])
+            sent_rows.at[d], got_rows.at[d], disp_send.at[at], disp_recv.at[at], peer(steps[d])
         )
 
-    @pl.when(core == 1)
-    def _():
-        disp_copy(0).start()
-
-    for d in range(1, nz):
-        disp_copy(d).start()
+    def slots_of(k, act):
+        for d in range(starts[k], starts[k] + SIZES[k]):
+            if d == home:
+                pl.when(core == 1)(functools.partial(act, d))
+            else:
+                act(d)
+
+    for k in SENDS:
+        slots_of(k, lambda d: disp_copy(d).start())
 
     @pl.when(core == 0)
     def _():
-        got_rows[0] = sent_rows[0]
+        got_rows[home] = sent_rows[home]
 
     win_copy.start()
     wout_copy.start()
@@ -239,82 +272,73 @@
         high.append(as_column((value >> 8).astype(F32)))
         low.append(as_column(jnp.bitwise_and(value, 255).astype(F32)))
     for k in range(CHUNKS):
-        lane = (lax.broadcasted_iota(jnp.int32, (count, rows), 1) + k * rows).astype(F32)
+        lane = (
+            lax.broadcasted_iota(jnp.int32, (count, counts[k]), 1) + starts[k] * CAP
+        ).astype(F32)
         for ref, part in ((pick_hi, high), (pick_lo, low)):
-            ref[k] = (
+            ref[k, :, : counts[k]] = (
                 jnp.where(lane == column[0], part[0], 0.0)
                 + jnp.where(lane == column[1], part[1], 0.0)
             ).astype(BF16)
 
-    sends = []
-
     def gat(k, i, ref, to):
-        copy = remote(ref, ref, gat_send.at[k, i], gat_recv.at[k, i], to)
-        copy.start()
-        sends.append(copy)
+        remote(ref, ref, gat_send.at[k], gat_recv.at[lane_of(GATHER, k, i)], to).start()
 
     def gat_wait(k, i, ref):
-        remote(ref, ref, gat_send.at[k, i], gat_recv.at[k, i], across).wait_recv()
+        took(gat_recv.at[lane_of(GATHER, k, i)], ref)
 
     def red(k, i, src, dst, to):
-        copy = remote(src, dst, red_send.at[k, i], red_recv.at[k, i], to)
-        copy.start()
-        sends.append(copy)
+        remote(src, dst, red_send.at[k], red_recv.at[lane_of(REDUCE, k, i)], to).start()
 
     def red_wait(k, i, ref):
-        remote(ref, ref, red_send.at[k, i], red_recv.at[k, i], across).wait_recv()
-
-    def slots_of(k, act):
-        for d in range(k * slots_chunk, (k + 1) * slots_chunk):
-            if d == 0:
-                pl.when(core == 1)(functools.partial(act, d))
-            else:
-                act(d)
+        took(red_recv.at[lane_of(REDUCE, k, i)], ref)
+
+    def piece_ref(k, q):
+        return held.at[k, q, whole[k]]
 
     def arrive(k):
-        slots_of(k, lambda d: disp_copy(d).wait_recv())
-        held[k, chip] = to_rows(got_rows[k * slots_chunk : (k + 1) * slots_chunk])
-        mine = held.at[k, chip]
+        per_chunk(k, lambda slots: took(disp_recv.at[k], got_rows.at[slots]))
+        held[k, chip, whole[k]] = to_rows(got_rows[spans[k]])
+        mine = piece_ref(k, chip)
         if GATHER[k] == "D":
-            for offset in DIRECT:
-                gat(k, offset - 1, mine, mate(offset))
+            for i, (dy, dx) in enumerate(DIRECT):
+                gat(k, i, mine, mate(dy, dx))
         else:
             gat(k, 0, mine, across)
             gat(k, 1, mine, right)
             gat(k, 2, mine, left)
 
     def arrive_across(k):
-        other = held.at[k, piece(y, 0)]
+        other = piece_ref(k, piece(y, 0))
         gat_wait(k, 0, other)
         gat(k, 3, other, right)
         gat(k, 4, other, left)
 
     def pass_on(k, a, from_left):
         i = 1 + 2 * (1 - a) + (0 if from_left else 1)
-        ref = held.at[k, piece(y_left if from_left else y_right, a)]
+        ref = piece_ref(k, piece(y_left if from_left else y_right, a))
         gat_wait(k, i, ref)
         gat(k, i + 4, ref.at[first if from_left else second], right if from_left else left)
         if GATHER[k] == "B":
             gat(k, i + 2, ref, across)
 
     def far_across(k):
-        far = held.at[k, piece(y_far, 1)]
+        far = piece_ref(k, piece(y_far, 1))
         gat_wait(k, 5, far.at[first])
         gat_wait(k, 6, far.at[second])
         gat(k, 7, far, across)
 
     def all_there(k):
         if GATHER[k] == "D":
-            for offset in range(1, CHIPS):
-                gat_wait(k, offset - 1, held.at[k, lax.rem(chip + CHIPS - offset, CHIPS)])
+            gat_wait(k, 0, held.at[k, pl.ds(0, CHIPS - 1), whole[k]])
         elif GATHER[k] == "B":
-            gat_wait(k, 0, held.at[k, piece(y, 0)])
-            gat_wait(k, 3, held.at[k, piece(y_left, 0)])
-            gat_wait(k, 4, held.at[k, piece(y_right, 0)])
-            gat_wait(k, 7, held.at[k, piece(y_far, 0)])
+            gat_wait(k, 0, piece_ref(k, piece(y, 0)))
+            gat_wait(k, 3, piece_ref(k, piece(y_left, 0)))
+            gat_wait(k, 4, piece_ref(k, piece(y_right, 0)))
+            gat_wait(k, 7, piece_ref(k, piece(y_far, 0)))
         else:
             for a in range(2):
-                far = held.at[k, piece(y_far, a)]
+                far = piece_ref(k, piece(y_far, a))
                 gat_wait(k, 7 - 2 * a, far.at[first])
                 gat_wait(k, 8 - 2 * a, far.at[second])
 
@@ -323,18 +347,19 @@
 
     def hidden(k):
         all_there(k)
-        sums = jnp.zeros((rows, WIDE), F32)
-        squares = jnp.zeros((rows, WIDE), F32)
+        rows = whole[k]
+        sums = jnp.zeros((counts[k], WIDE), F32)
+        squares = jnp.zeros((counts[k], WIDE), F32)
         for q in range(CHIPS):
-            x = held[k, q].astype(F32)
+            x = held[k, q, rows].astype(F32)
             sums += x
             squares += x * x
         mean = jnp.sum(sums, axis=1, keepdims=True) / D
         inverse = lax.rsqrt(jnp.sum(squares, axis=1, keepdims=True) / D - mean * mean + 1e-06)
         for q in range(CHIPS):
             at = slice(q * WIDE, (q + 1) * WIDE)
-            x = held[k, q].astype(F32)
-            normed[:, at] = (
+            x = held[k, q, rows].astype(F32)
+            normed[rows, at] = (
                 (x - mean) * inverse * (1.0 + scale[:, at]) + shift[:, at]
             ).astype(BF16)
         if not ready:
@@ -346,95 +371,94 @@
         for c in range(2):
             for t in range(tiles):
                 at = slice(t * WIDE, (t + 1) * WIDE)
-                h = jnp.dot(normed[...], win[c, :, at], preferred_element_type=F32)
-                hid[c, :, at] = jax.nn.gelu(h, approximate=True).astype(BF16)
-
-    def result(q):
+                h = jnp.dot(normed[rows, :], win[c, :, at], preferred_element_type=F32)
+                hid[c, rows, at] = jax.nn.gelu(h, approximate=True).astype(BF16)
+
+    def result(k, q):
         at = pl.ds(pl.multiple_of(q * WIDE, WIDE), WIDE)
-        return jnp.dot(hid[0], wout[0, :, at], preferred_element_type=F32) + jnp.dot(
-            hid[1], wout[1, :, at], preferred_element_type=F32
+        return jnp.dot(hid[0, whole[k]], wout[0, :, at], preferred_element_type=F32) + jnp.dot(
+            hid[1, whole[k]], wout[1, :, at], preferred_element_type=F32
         )
 
     def far_results(k, a):
-        far_out[k, a] = result(piece(y_far, a)).astype(BF16)
+        far_out[k, a, whole[k]] = result(k, piece(y_far, a)).astype(BF16)
         for i, (part, to) in enumerate(((first, right), (second, left))):
-            red(k, 2 * i + a, far_out.at[k, a, part], far_in.at[k, a, part], to)
+            src, dst = far_out.at[k, a, whole[k]].at[part], far_in.at[k, a, whole[k]].at[part]
+            red(k, 2 * i + a, src, dst, to)
 
     def near_results(k):
         for a in range(2):
-            part_near[a, 0] = result(piece(y_right, a))
-            part_near[a, 1] = result(piece(y_left, a))
+            part_near[a, 0, whole[k]] = result(k, piece(y_right, a))
+            part_near[a, 1, whole[k]] = result(k, piece(y_left, a))
 
     def own_results(k):
         if REDUCE[k] == "D":
-            part_own[k, 1] = result(chip)
+            part_own[k, 1, whole[k]] = result(k, chip)
         else:
             for a in range(2):
-                part_own[k, a] = result(piece(y, a))
+                part_own[k, a, whole[k]] = result(k, piece(y, a))
 
     def near_sum(k, a, i):
-        here, rest = (first, second) if i == 0 else (second, first)
-        red_wait(k, 2 * i + a, far_in.at[k, a, here])
-        near_out[k, a, i, here] = (
-            part_near[a, i, here] + far_in[k, a, here].astype(F32)
-        ).astype(BF16)
-        near_out[k, a, i, rest] = part_near[a, i, rest].astype(BF16)
+        here, rest = (0, LANES) if i == 0 else (LANES, 0)
+        got = far_in.at[k, a, whole[k]]
+        red_wait(k, 2 * i + a, got.at[first if i == 0 else second])
+        for at, add in ((pl.ds(here, LANES), True), (pl.ds(rest, LANES), False)):
+            value = part_near[a, i, whole[k], at]
+            if add:
+                value = value + far_in[k, a, whole[k], at].astype(F32)
+            near_out[k, a, i, whole[k], at] = value.astype(BF16)
         j = 4 + 2 * i + a
-        red(k, j, near_out.at[k, a, i], near_in.at[k, a, i], right if i == 0 else left)
+        src, dst = near_out.at[k, a, i, whole[k]], near_in.at[k, a, i, whole[k]]
+        red(k, j, src, dst, right if i == 0 else left)
 
     def own_sum(k, a):
-        value = part_own[k, a]
+        value = part_own[k, a, whole[k]]
         for i in range(2):
-            red_wait(k, 4 + 2 * i + a, near_in.at[k, a, i])
-            value = value + near_in[k, a, i].astype(F32)
+            red_wait(k, 4 + 2 * i + a, near_in.at[k, a, i, whole[k]])
+            value = value + near_in[k, a, i, whole[k]].astype(F32)
         return value
 
     def sum_across(k):
-        x_out[k] = own_sum(k, 0).astype(BF16)
-        red(k, 8, x_out.at[k], x_in.at[k], across)
-
-    def block_of(k, i, far, near, x):
-        if i < 2:
-            return far.at[k, i]
-        return near.at[k, (i - 2) // 2, (i - 2) % 2] if i < 6 else x.at[k]
+        x_out[k, whole[k]] = own_sum(k, 0).astype(BF16)
+        red(k, 8, x_out.at[k, whole[k]], x_in.at[k, whole[k]], across)
 
     def direct_results(k):
-        for offset in DIRECT:
-            src = block_of(k, offset - 1, far_out, near_out, x_out)
-            dst = block_of(k, offset - 1, far_in, near_in, x_in)
-            src[...] = result(lax.rem(chip + offset, CHIPS)).astype(BF16)
-            red(k, offset - 1, src, dst, mate(offset))
+        for i, (dy, dx) in enumerate(DIRECT):
+            src, dst = all_out.at[k, i, whole[k]], all_in.at[k, i, whole[k]]
+            src[...] = result(k, chip_at(dy, dx)).astype(BF16)
+            red(k, i, src, dst, mate(dy, dx))
 
     def back_copy(d):
+        at = chunk_of(d)
         return remote(
-            back_out.at[d], back_in.at[d], back_send.at[d], back_recv.at[d], peer(nz - steps[d])
+            back_out.at[d], back_in.at[d], back_send.at[at], back_recv.at[at], peer(nz - steps[d])
         )
 
     def give_back(k):
         if REDUCE[k] == "D":
-            value = part_own[k, 1]
+            value = part_own[k, 1, whole[k]]
+            red_wait(k, 0, all_in.at[k, :, whole[k]])
             for i in range(CHIPS - 1):
-                ref = block_of(k, i, far_in, near_in, x_in)
-                red_wait(k, i, ref)
-                value = value + ref[...].astype(F32)
+                value = value + all_in[k, i, whole[k]].astype(F32)
         else:
             value = own_sum(k, 1)
-            red_wait(k, 8, x_in.at[k])
-            value = value + x_in[k].astype(F32)
-        back_out[k * slots_chunk : (k + 1) * slots_chunk] = to_messages(value)
+            red_wait(k, 8, x_in.at[k, whole[k]])
+            value = value + x_in[k, whole[k]].astype(F32)
+        back_out[spans[k]] = to_messages(value)
         slots_of(k, lambda d: back_copy(d).start())
-        if k == 0:
+        if starts[k] <= home < starts[k] + SIZES[k]:
             @pl.when(core == 0)
             def _():
-                back_in[0] = back_out[0]
+                back_in[home] = back_out[home]
 
     begun = []
 
     def combine(k):
-        slots_of(k, lambda d: back_copy(d).wait_recv())
-        values = to_rows(back_in[k * slots_chunk : (k + 1) * slots_chunk])
-        part = 256.0 * jnp.dot(pick_hi[k], values, preferred_element_type=F32) + jnp.dot(
-            pick_lo[k], values, preferred_element_type=F32
+        per_chunk(k, lambda slots: took(back_recv.at[k], back_in.at[slots]))
+        values = to_rows(back_in[spans[k]])
+        at = slice(0, counts[k])
+        part = 256.0 * jnp.dot(pick_hi[k, :, at], values, preferred_element_type=F32) + jnp.dot(
+            pick_lo[k, :, at], values, preferred_element_type=F32
         )
         total[...] = total[...] + part if begun else part
         begun.append(k)
@@ -469,17 +493,19 @@
     comb[1] = answer[:, LANES:]
     comb_copy = remote(comb.at[1 - core], comb_in, one_send.at[3], one_recv.at[3], sibling)
     comb_copy.start()
-    for copy in [tok_copy, win_copy, wout_copy] + sends:
+    for copy in (tok_copy, win_copy, wout_copy):
         copy.wait_send()
     for k in range(CHUNKS):
-        slots_of(k, lambda d: disp_copy(d).wait_send())
-        slots_of(k, lambda d: back_copy(d).wait_send())
+        took(gat_send.at[k], held.at[k, pl.ds(0, CHIPS - 1), whole[k]])
+        took(red_send.at[k], all_out.at[k, :, whole[k]])
+        per_chunk(k, lambda slots: took(disp_send.at[k], sent_rows.at[slots]))
+        per_chunk(k, lambda slots: took(back_send.at[k], back_out.at[slots]))
     comb_copy.wait_recv()
     out[...] = (tok2[core].astype(F32) + gate[...] * (comb[core] + comb_in[...])).astype(BF16)
     comb_copy.wait_send()
 
 
-DIRECT = (2, 6, 1, 7, 3, 5, 4)
+DIRECT = ((2, 1), (1, 1), (3, 1), (2, 0), (0, 1), (1, 0), (3, 0))
 
 
 def shards(
@@ -489,7 +515,7 @@
     nz = n_tok // 2
     count = tokens.shape[0]
     units = weight_in.shape[2]
-    rows = nz // CHUNKS * CAP
+    rows = max(SIZES) * CAP
     hbm = pl.BlockSpec(memory_space=pltpu.HBM)
     dma = pltpu.SemaphoreType.DMA
     scratch = [
@@ -515,6 +541,8 @@
         pltpu.VMEM((CHUNKS, 2, 2, rows, WIDE), BF16),
         pltpu.VMEM((CHUNKS, rows, WIDE), BF16),
         pltpu.VMEM((CHUNKS, rows, WIDE), BF16),
+        pltpu.VMEM((CHUNKS, CHIPS - 1, rows, WIDE), BF16),
+        pltpu.VMEM((CHUNKS, CHIPS - 1, rows, WIDE), BF16),
         pltpu.VMEM((nz, 2 * CAP, LANES), BF16),
         pltpu.VMEM((nz, 2 * CAP, LANES), BF16),
         pltpu.VMEM((CHUNKS, count, rows), BF16),
@@ -525,14 +553,14 @@
         dma((9,)),
         dma((4,)),
         dma((4,)),
-        dma((nz,)),
-        dma((nz,)),
-        dma((CHUNKS, 9)),
-        dma((CHUNKS, 9)),
-        dma((CHUNKS, 9)),
-        dma((CHUNKS, 9)),
-        dma((nz,)),
-        dma((nz,)),
+        dma((CHUNKS,)),
+        dma((CHUNKS,)),
+        dma((CHUNKS,)),
+        dma((lane_of(GATHER, CHUNKS, 0),)),
+        dma((CHUNKS,)),
+        dma((lane_of(REDUCE, CHUNKS, 0),)),
+        dma((CHUNKS,)),
+        dma((CHUNKS,)),
     ]
     return pl.pallas_call(
         functools.partial(kernel, n_tok),
@@ -544,9 +572,9 @@
             collective_id=0, has_side_effects=True, vmem_limit_bytes=60 * 1024 * 1024
         ),
         cost_estimate=pl.CostEstimate(
-            flops=4 * 2 * rows * CHUNKS * D * units,
+            flops=4 * 2 * nz * CAP * D * units,
             bytes_accessed=4 * D * units,
-            transcendentals=2 * rows * CHUNKS * units,
+            transcendentals=2 * nz * CAP * units,
         ),
     )(
         tokens,

time: 71.3 us -> 67.1 us (0.941)
  Pallas kernels: 69.7 us -> 65.5 us
    pallas_call x1, Pallas kernels: 69.7 us -> 65.5 us  [shards(): pl.pallas_call(functools.partial(kernel, n_tok), out_shape=jax.ShapeDtype...]
where the time goes in v3:
time: 67.1 us; the launch traced here: 67 us
  Pallas kernels  65.5 us (98%)
  local copies, waits for them, and re-layouts  1.47 us (2%)
    pallas_call x1, Pallas kernels, shards(): pl.pallas_call(functools.partial(kernel, n_tok), out_shape=jax.ShapeDtype...  65.5 us
    unnamed x1, local copies, waits for them, and re-layouts  1.47 us

profile of v3, /device:TPU:1, one launch (start us, length us, event | category | flops | bytes accessed | tf_op | source)
XLA Modules:
  0.0 67.0 jit_solution(16007910338972411271)
XLA Ops:
  0.0 65.5 %shard_map.91 = bf16[256,128]{1,0:T(8,128)(2,1)} custom-call(bf16[256,128]{1,0:T(8,128)(2,1)} %tokens_hbm.1, f32[1,2048]{1,0:T(1,128)} %bitcast.6, f32[1,2048]{1,0:T(1,128)} %bitcast.7, f32[1,2048]{1,0:T(1,128)} %bitcast.8, s32[2,256]{1,0:T(2,128)} %bitcast.9, s32[2,256]{1,0:T(2,128)} %bitcast.10, s32[1,32]{1,0:T(1,128)} %bitcast.11, ...), custom_call_target="tpu_custom_call" | custom-call | flops 3221225472 | bytes 4194304 | tf_op jit(solution)/shard_map/pallas_call | solution.py:565
  65.5 1.5 %copy.11 = bf16[256,128]{1,0:T(8,128)(2,1)} copy(bf16[256,128]{1,0:T(8,128)(2,1)} %shard_map.91) | data formatting | bytes 131072

commit v4 on v3

--- a/solution.py
+++ b/solution.py
@@ -41,8 +41,12 @@
     )
 
 
+SHARED = {"D": (0,) * 7, "B": (0, 1, 2, 0, 0, 3, 3, 0), "A": (0, 1, 2, 3, 4, 5, 4, 5, 5)}
+
+
 def lane_of(kinds, k, i):
-    return sum(1 if kind == "D" else 9 for kind in kinds[:k]) + (0 if kinds[k : k + 1] == "D" else i)
+    before = sum(max(SHARED[kind]) + 1 for kind in kinds[:k])
+    return before + (SHARED[kinds[k]][i] if k < len(kinds) else 0)
 
 
 def to_rows(block):
@@ -240,7 +244,7 @@
     def disp_copy(d):
         at = chunk_of(d)
         return remote(
-            sent_rows.at[d], got_rows.at[d], disp_send.at[at], disp_recv.at[at], peer(steps[d])
+            sent_rows.at[d], got_rows.at[d], disp_send.at[0], disp_recv.at[at], peer(steps[d])
         )
 
     def slots_of(k, act):
@@ -282,13 +286,13 @@
             ).astype(BF16)
 
     def gat(k, i, ref, to):
-        remote(ref, ref, gat_send.at[k], gat_recv.at[lane_of(GATHER, k, i)], to).start()
+        remote(ref, ref, gat_send.at[0], gat_recv.at[lane_of(GATHER, k, i)], to).start()
 
     def gat_wait(k, i, ref):
         took(gat_recv.at[lane_of(GATHER, k, i)], ref)
 
     def red(k, i, src, dst, to):
-        remote(src, dst, red_send.at[k], red_recv.at[lane_of(REDUCE, k, i)], to).start()
+        remote(src, dst, red_send.at[0], red_recv.at[lane_of(REDUCE, k, i)], to).start()
 
     def red_wait(k, i, ref):
         took(red_recv.at[lane_of(REDUCE, k, i)], ref)
@@ -324,18 +328,14 @@
 
     def far_across(k):
         far = piece_ref(k, piece(y_far, 1))
-        gat_wait(k, 5, far.at[first])
-        gat_wait(k, 6, far.at[second])
+        gat_wait(k, 5, far)
         gat(k, 7, far, across)
 
     def all_there(k):
         if GATHER[k] == "D":
             gat_wait(k, 0, held.at[k, pl.ds(0, CHIPS - 1), whole[k]])
         elif GATHER[k] == "B":
-            gat_wait(k, 0, piece_ref(k, piece(y, 0)))
-            gat_wait(k, 3, piece_ref(k, piece(y_left, 0)))
-            gat_wait(k, 4, piece_ref(k, piece(y_right, 0)))
-            gat_wait(k, 7, piece_ref(k, piece(y_far, 0)))
+            gat_wait(k, 0, held.at[k, pl.ds(0, 4), whole[k]])
         else:
             for a in range(2):
                 far = piece_ref(k, piece(y_far, a))
@@ -413,8 +413,8 @@
 
     def own_sum(k, a):
         value = part_own[k, a, whole[k]]
+        red_wait(k, 4 + a, all_in.at[k, pl.ds(0, 2 + a), whole[k]])
         for i in range(2):
-            red_wait(k, 4 + 2 * i + a, near_in.at[k, a, i, whole[k]])
             value = value + near_in[k, a, i, whole[k]].astype(F32)
         return value
 
@@ -431,7 +431,7 @@
     def back_copy(d):
         at = chunk_of(d)
         return remote(
-            back_out.at[d], back_in.at[d], back_send.at[at], back_recv.at[at], peer(nz - steps[d])
+            back_out.at[d], back_in.at[d], back_send.at[0], back_recv.at[at], peer(nz - steps[d])
         )
 
     def give_back(k):
@@ -442,7 +442,6 @@
                 value = value + all_in[k, i, whole[k]].astype(F32)
         else:
             value = own_sum(k, 1)
-            red_wait(k, 8, x_in.at[k, whole[k]])
             value = value + x_in[k, whole[k]].astype(F32)
         back_out[spans[k]] = to_messages(value)
         slots_of(k, lambda d: back_copy(d).start())
@@ -495,11 +494,15 @@
     comb_copy.start()
     for copy in (tok_copy, win_copy, wout_copy):
         copy.wait_send()
-    for k in range(CHUNKS):
-        took(gat_send.at[k], held.at[k, pl.ds(0, CHIPS - 1), whole[k]])
-        took(red_send.at[k], all_out.at[k, :, whole[k]])
-        per_chunk(k, lambda slots: took(disp_send.at[k], sent_rows.at[slots]))
-        per_chunk(k, lambda slots: took(back_send.at[k], back_out.at[slots]))
+    took(gat_send.at[0], all_out)
+    took(red_send.at[0], all_out)
+
+    def sent(slots):
+        took(disp_send.at[0], sent_rows.at[slots])
+        took(back_send.at[0], back_out.at[slots])
+
+    pl.when(core == 1)(lambda: sent(pl.ds(0, nz)))
+    pl.when(core == 0)(lambda: sent(pl.ds(1, nz - 1)))
     comb_copy.wait_recv()
     out[...] = (tok2[core].astype(F32) + gate[...] * (comb[core] + comb_in[...])).astype(BF16)
     comb_copy.wait_send()
@@ -553,13 +556,13 @@
         dma((9,)),
         dma((4,)),
         dma((4,)),
+        dma((1,)),
         dma((CHUNKS,)),
-        dma((CHUNKS,)),
-        dma((CHUNKS,)),
+        dma((1,)),
         dma((lane_of(GATHER, CHUNKS, 0),)),
-        dma((CHUNKS,)),
+        dma((1,)),
         dma((lane_of(REDUCE, CHUNKS, 0),)),
-        dma((CHUNKS,)),
+        dma((1,)),
         dma((CHUNKS,)),
     ]
     return pl.pallas_call(

time: 67.1 us -> 66.9 us (level)
  no operation moved by 1% of the time
where the time goes in v4:
time: 66.9 us; the launch traced here: 66.8 us
  Pallas kernels  65.3 us (98%)
  local copies, waits for them, and re-layouts  1.47 us (2%)
    pallas_call x1, Pallas kernels, shards(): pl.pallas_call(functools.partial(kernel, n_tok), out_shape=jax.ShapeDtype...  65.3 us
    unnamed x1, local copies, waits for them, and re-layouts  1.47 us

profile of v4, /device:TPU:1, one launch (start us, length us, event | category | flops | bytes accessed | tf_op | source)
XLA Modules:
  0.0 66.8 jit_solution(1192075552487054964)
XLA Ops:
  0.0 65.3 %shard_map.91 = bf16[256,128]{1,0:T(8,128)(2,1)} custom-call(bf16[256,128]{1,0:T(8,128)(2,1)} %tokens_hbm.1, f32[1,2048]{1,0:T(1,128)} %bitcast.6, f32[1,2048]{1,0:T(1,128)} %bitcast.7, f32[1,2048]{1,0:T(1,128)} %bitcast.8, s32[2,256]{1,0:T(2,128)} %bitcast.9, s32[2,256]{1,0:T(2,128)} %bitcast.10, s32[1,32]{1,0:T(1,128)} %bitcast.11, ...), custom_call_target="tpu_custom_call" | custom-call | flops 3221225472 | bytes 4194304 | tf_op jit(solution)/shard_map/pallas_call | solution.py:568
  65.3 1.5 %copy.11 = bf16[256,128]{1,0:T(8,128)(2,1)} copy(bf16[256,128]{1,0:T(8,128)(2,1)} %shard_map.91) | data formatting | bytes 131072
